TPU v7x, 512 devices: a whole 4x8x8 slice. The times are simulated.
512 devices in a mesh: seq: 32 (over z_hi, y, core), tensor: 16 (over x, z_lo).
Axes of the slice: x: 4, y: 8, z: 8 (z_hi: 2, z_lo: 4; z = z_hi * 4 + z_lo), core: 2. Of those that a mesh axis runs over, the one named last changes fastest.
Arguments:
- hidden_in: bfloat16 [8192, 5376], P('seq', 'tensor'), may hold values from -128 to 128
- positions: int32 [8192], P('seq'), may hold values from 0 to 16382, as said below
- pre_gain: float32 [5376], replicated, may hold values from -0.5 to 1.5
- query_weight: bfloat16 [5376, 4096], P('seq', 'tensor')
- key_weight: bfloat16 [5376, 2048], P('seq', 'tensor')
- value_weight: bfloat16 [5376, 2048], P('seq', 'tensor'), may hold values from -0.078125 to 0.078125
- query_gain: float32 [128], replicated, may hold values from -0.3 to 4.5
- key_gain: float32 [128], replicated, may hold values from -0.3 to 4.5
- output_weight: bfloat16 [4096, 5376], P('tensor', 'seq')
- post_gain: float32 [5376], P('tensor'), may hold values from -0.5 to 1.5
Outputs:
- hidden_out: bfloat16 [8192, 5376], P('seq', 'tensor')
Inputs may be any that keep to these rules, and one draw needn't show every extreme that they name: `positions`: 0 at a prompt's first token, else one more than the position of the token before; the window's first token continues a prompt begun before the window, and some later token starts a new prompt.
All inputs are finite; a program needn't handle non-finite values.
Results may differ from a plain program's by a relative error of at most 0.013.
Values may be sent and summed in bfloat16 or wider, within the bound.
A program may use at most 64 MiB of HBM per device.

v0:
```python
import jax
import jax.numpy as jnp
from jax import lax
from jax.sharding import PartitionSpec as P

WINDOW = 1024
epsilon = 1e-06
query_scalar = 168.0
rope_base = 10000.0
masked_score = -1e30


def passed_along(value, axis, steps):
    count = lax.axis_size(axis)
    initial, last = (max(0, -steps), min(count, count - steps))
    return lax.ppermute(value, axis, [(source, source + steps) for source in range(initial, last)])


def rms_scale(values):
    return values * lax.rsqrt(jnp.mean(values * values, axis=-1, keepdims=True) + epsilon)


def rotary(values, token_positions):
    half_dim = values.shape[-1] // 2
    exponent = jnp.arange(half_dim, dtype=jnp.float32) * 2.0 / values.shape[-1]
    inverse = 1.0 / rope_base**exponent
    angles = token_positions.astype(jnp.float32)[:, None] * inverse[None, :]
    cosine = jnp.cos(angles)[:, None, :]
    sine = jnp.sin(angles)[:, None, :]
    first_half = values[..., :half_dim]
    second_half = values[..., half_dim:]
    return jnp.concatenate(
        [first_half * cosine - second_half * sine, second_half * cosine + first_half * sine],
        axis=-1,
    )


def body(
    hidden_in,
    positions,
    pre_gain,
    query_weight,
    key_weight,
    value_weight,
    query_gain,
    key_gain,
    output_weight,
    post_gain,
):
    tokens_dev = hidden_in.shape[0]
    width_dev = hidden_in.shape[1]
    head_dim = query_gain.shape[0]
    kv_local = key_weight.shape[1] // head_dim
    whole = lax.all_gather(hidden_in, "tensor", axis=1, tiled=True)
    normed = (rms_scale(whole.astype(jnp.float32)) * (1.0 + pre_gain)).astype(jnp.bfloat16)

    def accumulate(piece):
        return jnp.dot(normed, piece, preferred_element_type=jnp.float32)

    query_sum = accumulate(lax.all_gather(query_weight, "seq", axis=0, tiled=True))
    key_sum = accumulate(lax.all_gather(key_weight, "seq", axis=0, tiled=True))
    value_sum = accumulate(lax.all_gather(value_weight, "seq", axis=0, tiled=True))
    queries = rotary(
        rms_scale(query_sum.reshape(tokens_dev, -1, head_dim)) * (1.0 + query_gain), positions
    )
    queries = queries.astype(jnp.bfloat16).reshape(tokens_dev, kv_local, 2, head_dim)
    key_own = rotary(
        rms_scale(key_sum.reshape(tokens_dev, kv_local, head_dim)) * (1.0 + key_gain), positions
    ).astype(jnp.bfloat16)
    value_own = value_sum.reshape(tokens_dev, kv_local, head_dim).astype(jnp.bfloat16)
    reach = (WINDOW + tokens_dev - 2) // tokens_dev
    earlier = []
    for distance in range(reach, 0, -1):
        earlier.append(passed_along((key_own, value_own), "seq", distance))
    key_rows = jnp.concatenate([pair[0] for pair in earlier] + [key_own], axis=0)
    value_rows = jnp.concatenate([pair[1] for pair in earlier] + [value_own], axis=0)
    seq_index = lax.axis_index("seq")
    query_index = seq_index * tokens_dev + jnp.arange(tokens_dev, dtype=jnp.int32)
    key_index = (seq_index - reach) * tokens_dev + jnp.arange(key_rows.shape[0], dtype=jnp.int32)
    gap = query_index[:, None] - key_index[None, :]
    allowed = (gap >= 0) & (gap < WINDOW) & (gap <= positions[:, None]) & (key_index >= 0)[None, :]
    scores = jnp.einsum(
        "qgrd,kgd->grqk", queries, key_rows, preferred_element_type=jnp.float32
    ) * query_scalar ** (-0.5)
    scores = jnp.where(allowed[None, None], scores, masked_score)
    peak = jnp.max(scores, axis=-1, keepdims=True)
    expo = jnp.exp(scores - peak)
    weights = (expo / jnp.sum(expo, axis=-1, keepdims=True)).astype(jnp.bfloat16)
    context = jnp.einsum("grqk,kgd->qgrd", weights, value_rows, preferred_element_type=jnp.float32)
    context = context.astype(jnp.bfloat16).reshape(tokens_dev, -1)
    term = jnp.dot(
        context,
        lax.all_gather(output_weight, "seq", axis=1, tiled=True),
        preferred_element_type=jnp.float32,
    )
    share = lax.psum_scatter(
        term.astype(jnp.bfloat16), "tensor", scatter_dimension=1, tiled=True
    ).astype(jnp.float32)
    squares = lax.psum(jnp.sum(share * share, axis=-1), "tensor")
    mean_square = squares / (width_dev * lax.axis_size("tensor"))
    post = share * lax.rsqrt(mean_square[:, None] + epsilon) * (1.0 + post_gain)
    return (hidden_in.astype(jnp.float32) + post).astype(jnp.bfloat16)


def solution(mesh):
    placed = (
        P("seq", "tensor"),
        P("seq"),
        P(),
        P("seq", "tensor"),
        P("seq", "tensor"),
        P("seq", "tensor"),
        P(),
        P(),
        P("tensor", "seq"),
        P("tensor"),
    )
    return jax.shard_map(
        body, mesh=mesh, in_specs=placed, out_specs=P("seq", "tensor"), check_vma=False
    )
```

profile of v0, /device:TPU:16, one launch (start us, length us, event | category | flops | bytes accessed | tf_op | source)
XLA Modules:
  0.0 622.8 jit_solution(4040736795534656457)
XLA Ops:
  13.3 1.6 fusion.10
  14.9 93.1 %all-gather.6.cloned.1.call-done = bf16[256,5376]{0,1:T(8,128)(2,1)} async-done(((bf16[256,336]{0,1:T(8,128)(2,1)}), bf16[256,5376]{0,1:T(8,128)(2,1)}) %all-gather.6.cloned.1.call-update) | async-done | bytes 2752528 | tf_op jit(solution)/shard_map/all_gather | solution.py:54
  108.0 2.7 fusion
  110.7 87.3 %all-gather.10.cloned.1.call-done = bf16[5376,128]{1,0:T(8,128)(2,1)} async-done(((bf16[168,128]{1,0:T(8,128)(2,1)}), bf16[5376,128]{1,0:T(8,128)(2,1)}) %all-gather.10.cloned.1.call-update) | async-done | bytes 1376272 | tf_op jit(solution)/shard_map/all_gather | solution.py:61
  197.9 2.7 multiply_reduce_fusion.1
  201.1 3.8 collective-permute-start.4
  204.9 2.8 collective-permute-start.5
  207.7 3.4 collective-permute-start.6
  211.1 2.3 collective-permute-start.7
  213.4 73.1 %all-gather.8.cloned.1.call-done = bf16[5376,128]{1,0:T(8,128)(2,1)} async-done(((bf16[168,128]{1,0:T(8,128)(2,1)}), bf16[5376,128]{1,0:T(8,128)(2,1)}) %all-gather.8.cloned.1.call-update) | async-done | bytes 1376272 | tf_op jit(solution)/shard_map/all_gather | solution.py:62
  286.6 3.1 fusion.14
  289.6 3.8 collective-permute-start
  293.4 2.8 collective-permute-start.1
  297.7 3.4 collective-permute-start.2
  302.6 2.3 collective-permute-start.3
  310.8 71.3 %all-gather.12.cloned.1.call-done = bf16[5376,256]{1,0:T(8,128)(2,1)} async-done(((bf16[168,256]{1,0:T(8,128)(2,1)}), bf16[5376,256]{1,0:T(8,128)(2,1)}) %all-gather.12.cloned.1.call-update) | async-done | bytes 2752528 | tf_op jit(solution)/shard_map/all_gather | solution.py:60
  382.1 4.2 multiply_reduce_fusion
  387.7 1.6 fusion.38
  389.7 1.6 fusion.11
  391.3 85.6 %all-gather.14.cloned.1.call-done = bf16[256,5376]{0,1:T(8,128)(2,1)} async-done(((bf16[256,168]{0,1:T(8,128)(2,1)}), bf16[256,5376]{0,1:T(8,128)(2,1)}) %all-gather.14.cloned.1.call-update) | async-done | bytes 2752528 | tf_op jit(solution)/shard_map/all_gather | solution.py:93
  476.9 4.2 convolution_convert_fusion
  481.8 91.6 %reduce-scatter.2.cloned.1.call-done = bf16[256,336]{0,1:T(8,128)(2,1)} async-done(((bf16[256,5376]{0,1:T(8,128)(2,1)}), bf16[256,336]{0,1:T(8,128)(2,1)}) %reduce-scatter.2.cloned.1.call-update) | async-done | bytes 172048 | tf_op jit(solution)/shard_map/reduce_scatter | solution.py:96
  574.4 39.8 %psum.7 = f32[256]{0:T(256)S(1)} all-reduce(f32[256]{0:T(256)S(1)} %fusion.15), channel_id=1, replica_groups=mesh['seq'=32,'tensor'=16] {'tensor'}, use_global_device_ids=true, to_apply=%region_7.8 | all-reduce | flops 256 | bytes 2048 | tf_op jit(solution)/shard_map/psum | solution.py:99
  614.2 1.7 fusion.18
  (60 shorter events, 19.4 us)
Async XLA Ops:
  6.5 101.5 %all-gather.6.cloned.1.call-start = ((), (), s32[]{:S(2)}) async-start(), calls=%async_computation.1 | async-start | bytes 2924544 | tf_op jit(solution)/shard_map/all_gather | solution.py:54
  7.3 190.7 %all-gather.10.cloned.1.call-start = ((), (), s32[]{:S(2)}) async-start(), calls=%async_computation.3 | async-start | bytes 1419264 | tf_op jit(solution)/shard_map/all_gather | solution.py:61
  8.0 278.6 %all-gather.8.cloned.1.call-start = ((), (), s32[]{:S(2)}) async-start(), calls=%async_computation.2 | async-start | bytes 1419264 | tf_op jit(solution)/shard_map/all_gather | solution.py:62
  8.7 373.4 %all-gather.12.cloned.1.call-start = ((), (), s32[]{:S(2)}) async-start(), calls=%async_computation.4 | async-start | bytes 2838528 | tf_op jit(solution)/shard_map/all_gather | solution.py:60
  9.3 467.6 %all-gather.14.cloned.1.call-start = ((), (), s32[]{:S(2)}) async-start(), calls=%async_computation.5 | async-start | bytes 2838528 | tf_op jit(solution)/shard_map/all_gather | solution.py:93
  9.9 563.5 %reduce-scatter.2.cloned.1.call-start = ((), (), s32[]{:S(2)}) async-start(), calls=%async_computation.6 | async-start | bytes 2924544 | tf_op jit(solution)/shard_map/reduce_scatter | solution.py:96
  10.7 189.9 %copy-start.2 = (f32[5376]{0:T(1024)}, f32[5376]{0:T(1024)S(1)}, u32[]{:S(2)}) copy-start(f32[5376]{0:T(1024)S(1)} %broadcast_add_fusion) | copy-start | bytes 64516
  108.0 89.9 %copy-start = (bf16[256,5376]{0,1:T(8,128)(2,1)S(1)}, bf16[256,5376]{0,1:T(8,128)(2,1)}, u32[]{:S(2)}) copy-start(bf16[256,5376]{0,1:T(8,128)(2,1)} %all-gather.6.cloned.1.call-done) | copy-start | bytes 8257540
  201.1 92.3 %collective-permute-start.4 = (bf16[256,1,128]{0,2,1:T(8,128)(2,1)S(1)}, bf16[256,1,128]{0,2,1:T(8,128)(2,1)}, u32[]{:S(2)}, u32[]{:S(2)}) collective-permute-start(bf16[256,1,128]{0,2,1:T(8,128)(2,1)S(1)} %pad_maximum_fusion), channel_id=1, source_target_pairs={{0,64},{16,80},{32,96},{48,112},{64,128},{80,144},{96,160},{112,17... | collective-permute-start | bytes 196616 | tf_op jit(solution)/shard_map/ppermute | solution.py:16
  204.9 92.8 %collective-permute-start.5 = (bf16[256,1,128]{0,2,1:T(8,128)(2,1)S(1)}, bf16[256,1,128]{0,2,1:T(8,128)(2,1)}, u32[]{:S(2)}, u32[]{:S(2)}) collective-permute-start(bf16[256,1,128]{0,2,1:T(8,128)(2,1)S(1)} %pad_maximum_fusion), channel_id=1, source_target_pairs={{0,48},{16,64},{32,80},{48,96},{64,112},{80,128},{96,144},{112,160... | collective-permute-start | bytes 196616 | tf_op jit(solution)/shard_map/ppermute | solution.py:16
  207.7 94.9 %collective-permute-start.6 = (bf16[256,1,128]{0,2,1:T(8,128)(2,1)S(1)}, bf16[256,1,128]{0,2,1:T(8,128)(2,1)}, u32[]{:S(2)}, u32[]{:S(2)}) collective-permute-start(bf16[256,1,128]{0,2,1:T(8,128)(2,1)S(1)} %pad_maximum_fusion), channel_id=1, source_target_pairs={{0,32},{16,48},{32,64},{48,80},{64,96},{80,112},{96,128},{112,144}... | collective-permute-start | bytes 196616 | tf_op jit(solution)/shard_map/ppermute | solution.py:16
  211.1 95.2 %collective-permute-start.7 = (bf16[256,1,128]{0,2,1:T(8,128)(2,1)S(1)}, bf16[256,1,128]{0,2,1:T(8,128)(2,1)S(1)}, u32[]{:S(2)}, u32[]{:S(2)}) collective-permute-start(bf16[256,1,128]{0,2,1:T(8,128)(2,1)S(1)} %pad_maximum_fusion), channel_id=1, source_target_pairs={{0,16},{16,32},{32,48},{48,64},{64,80},{80,96},{96,112},{112,128},... | collective-permute-start | bytes 196616 | tf_op jit(solution)/shard_map/ppermute | solution.py:16
  289.6 18.0 %collective-permute-start = (bf16[256,1,128]{2,0,1:T(8,128)(2,1)S(1)}, bf16[256,1,128]{2,0,1:T(8,128)(2,1)S(1)}, u32[]{:S(2)}, u32[]{:S(2)}) collective-permute-start(bf16[256,1,128]{2,0,1:T(8,128)(2,1)S(1)} %fusion.14), channel_id=1, source_target_pairs={{0,64},{16,80},{32,96},{48,112},{64,128},{80,144},{96,160},{112,17... | collective-permute-start | bytes 196616 | tf_op jit(solution)/shard_map/ppermute | solution.py:16
  293.4 14.9 %collective-permute-start.1 = (bf16[256,1,128]{2,0,1:T(8,128)(2,1)S(1)}, bf16[256,1,128]{2,0,1:T(8,128)(2,1)S(1)}, u32[]{:S(2)}, u32[]{:S(2)}) collective-permute-start(bf16[256,1,128]{2,0,1:T(8,128)(2,1)S(1)} %fusion.14), channel_id=1, source_target_pairs={{0,48},{16,64},{32,80},{48,96},{64,112},{80,128},{96,144},{112,160... | collective-permute-start | bytes 196616 | tf_op jit(solution)/shard_map/ppermute | solution.py:16
  297.7 11.2 %collective-permute-start.2 = (bf16[256,1,128]{2,0,1:T(8,128)(2,1)S(1)}, bf16[256,1,128]{2,0,1:T(8,128)(2,1)S(1)}, u32[]{:S(2)}, u32[]{:S(2)}) collective-permute-start(bf16[256,1,128]{2,0,1:T(8,128)(2,1)S(1)} %fusion.14), channel_id=1, source_target_pairs={{0,32},{16,48},{32,64},{48,80},{64,96},{80,112},{96,128},{112,144}... | collective-permute-start | bytes 196616 | tf_op jit(solution)/shard_map/ppermute | solution.py:16
  302.6 6.9 %collective-permute-start.3 = (bf16[256,1,128]{2,0,1:T(8,128)(2,1)S(1)}, bf16[256,1,128]{2,0,1:T(8,128)(2,1)S(1)}, u32[]{:S(2)}, u32[]{:S(2)}) collective-permute-start(bf16[256,1,128]{2,0,1:T(8,128)(2,1)S(1)} %fusion.14), channel_id=1, source_target_pairs={{0,16},{16,32},{32,48},{48,64},{64,80},{80,96},{96,112},{112,128},... | collective-permute-start | bytes 196616 | tf_op jit(solution)/shard_map/ppermute | solution.py:16
  481.2 0.7 copy-start.3
  481.2 133.1 %copy-start.1 = (bf16[256,336]{0,1:T(8,128)(2,1)S(1)}, bf16[256,336]{0,1:T(8,128)(2,1)}, u32[]{:S(2)}) copy-start(bf16[256,336]{0,1:T(8,128)(2,1)} %param.10) | copy-start | bytes 516100
Sparse Core Ops, SparseCore 0:
  9.4 98.5 all-gather.5
  111.2 86.6 all-gather.9
  201.2 85.3 all-gather.7
  289.6 92.4 all-gather.11
  385.2 91.6 all-gather.13
  481.3 92.0 reduce-scatter.1
where the time goes:
time: 624 us; the launch traced here: 623 us
  waiting for transfers between devices  505 us (81%)
  blocking collectives  39.8 us (6%)
  starting transfers between devices  24.7 us (4%)
  matrix products  17.4 us (3%)
  between operations  13.7 us (2%)
  other arithmetic  12 us (2%)
  local copies, waits for them, and re-layouts  10 us (2%)
    all_gather x1, waiting for transfers between devices, body(): whole = lax.all_gather(hidden_in, 'tensor', axis=1, tiled=True)  93.1 us
    reduce_scatter x1, waiting for transfers between devices, body(): lax.psum_scatter(term.astype(jnp.bfloat16), 'tensor', scatter_dimension=1...  91.6 us
    all_gather x1, waiting for transfers between devices, body(): key_sum = accumulate(lax.all_gather(key_weight, 'seq', axis=0, tiled=True))  87.3 us
    all_gather x1, waiting for transfers between devices, body(): lax.all_gather(output_weight, 'seq', axis=1, tiled=True)  85.6 us
    all_gather x1, waiting for transfers between devices, body(): lax.all_gather(value_weight, 'seq', axis=0, tiled=True)  73.1 us
    all_gather x1, waiting for transfers between devices, body(): lax.all_gather(query_weight, 'seq', axis=0, tiled=True)  71.3 us
    psum x1, blocking collectives, body(): squares = lax.psum(jnp.sum(share * share, axis=-1), 'tensor')  39.8 us
    ppermute x8, starting transfers between devices, passed_along(): lax.ppermute(value, axis, [(source, source + steps) for source in range(i...  24.5 us
  transfers between devices with their start and end apart: 14, of which 6 were waited for; matrix products, arithmetic and copies ran while one was open for 5% of the time, Pallas kernels for 0%

commit v1 on v0

--- a/solution.py
+++ b/solution.py
@@ -8,6 +8,13 @@
 query_scalar = 168.0
 rope_base = 10000.0
 masked_score = -1e30
+
+
+def gather_over(array, mesh_axis, d):
+    peers = lax.axis_size(mesh_axis)
+    tiles = jnp.stack([array for _ in range(peers)])
+    tiles = lax.all_to_all(tiles, mesh_axis, split_axis=0, concat_axis=0)
+    return jnp.concatenate(tiles, axis=d)
 
 
 def passed_along(value, axis, steps):
@@ -57,7 +64,7 @@
     def accumulate(piece):
         return jnp.dot(normed, piece, preferred_element_type=jnp.float32)
 
-    query_sum = accumulate(lax.all_gather(query_weight, "seq", axis=0, tiled=True))
+    query_sum = accumulate(gather_over(query_weight, "seq", 0))
     key_sum = accumulate(lax.all_gather(key_weight, "seq", axis=0, tiled=True))
     value_sum = accumulate(lax.all_gather(value_weight, "seq", axis=0, tiled=True))
     queries = rotary(

time: 624 us -> 591 us (0.947)
  the two profiles are of different devices: /device:TPU:16 before, /device:TPU:32 now
where the time goes in v1:
time: 591 us
  waiting for transfers between devices  464 us (79%)
  blocking collectives  40.5 us (7%)
  starting transfers between devices  37.3 us (6%)
  matrix products  17.5 us (3%)
  between operations  13.5 us (2%)
  local copies, waits for them, and re-layouts  10.4 us (2%)
  other arithmetic  7.47 us (1%)
    all_gather x1, waiting for transfers between devices, body(): whole = lax.all_gather(hidden_in, 'tensor', axis=1, tiled=True)  138 us
    reduce_scatter x1, waiting for transfers between devices, body(): lax.psum_scatter(term.astype(jnp.bfloat16), 'tensor', scatter_dimension=1...  92.8 us
    all_gather x1, waiting for transfers between devices, body(): key_sum = accumulate(lax.all_gather(key_weight, 'seq', axis=0, tiled=True))  85.9 us
    all_gather x1, waiting for transfers between devices, body(): lax.all_gather(value_weight, 'seq', axis=0, tiled=True)  74.8 us
    all_gather x1, waiting for transfers between devices, body(): lax.all_gather(output_weight, 'seq', axis=1, tiled=True)  67.2 us
    psum x1, blocking collectives, body(): squares = lax.psum(jnp.sum(share * share, axis=-1), 'tensor')  40.5 us
    ppermute x8, starting transfers between devices, passed_along(): lax.ppermute(value, axis, [(source, source + steps) for source in range(i...  21.2 us
    all_to_all x1, starting transfers between devices, gather_over(): tiles = lax.all_to_all(tiles, mesh_axis, split_axis=0, concat_axis=0)  16 us
  transfers between devices with their start and end apart: 14, of which 8 were waited for; matrix products, arithmetic and copies ran while one was open for 5% of the time, Pallas kernels for 0%

profile of v1, /device:TPU:32, one launch (start us, length us, event | category | flops | bytes accessed | tf_op | source)
XLA Modules:
  0.0 590.8 jit_solution(18371298373084979569)
XLA Ops:
  8.7 2.6 stack.2
  11.4 16.0 %all-to-all-start = ((bf16[32,168,256]{2,1,0:T(8,128)(2,1)}), bf16[32,168,256]{2,1,0:T(8,128)(2,1)S(1)}, u32[]{:S(2)}, u32[]{:S(2)}) async-start(bf16[32,168,256]{2,1,0:T(8,128)(2,1)} %stack.2), calls=%async_computation | async-start | bytes 5505024 | tf_op jit(solution)/shard_map/all_to_all | solution.py:16
  29.4 137.9 %all-gather.5.cloned.1.call-done = bf16[256,5376]{0,1:T(8,128)(2,1)} async-done(((bf16[256,336]{0,1:T(8,128)(2,1)}), bf16[256,5376]{0,1:T(8,128)(2,1)}) %all-gather.5.cloned.1.call-update) | async-done | bytes 2752528 | tf_op jit(solution)/shard_map/all_gather | solution.py:61
  167.3 2.5 fusion
  169.8 85.9 %all-gather.9.cloned.1.call-done = bf16[5376,128]{1,0:T(8,128)(2,1)} async-done(((bf16[168,128]{1,0:T(8,128)(2,1)}), bf16[5376,128]{1,0:T(8,128)(2,1)}) %all-gather.9.cloned.1.call-update) | async-done | bytes 1376272 | tf_op jit(solution)/shard_map/all_gather | solution.py:68
  255.7 3.6 multiply_reduce_fusion.1
  259.7 4.2 collective-permute-start.4
  264.0 2.1 collective-permute-start.5
  266.1 2.4 collective-permute-start.6
  268.4 1.9 collective-permute-start.7
  270.4 74.8 %all-gather.7.cloned.1.call-done = bf16[5376,128]{1,0:T(8,128)(2,1)} async-done(((bf16[168,128]{1,0:T(8,128)(2,1)}), bf16[5376,128]{1,0:T(8,128)(2,1)}) %all-gather.7.cloned.1.call-update) | async-done | bytes 1376272 | tf_op jit(solution)/shard_map/all_gather | solution.py:69
  345.2 3.9 fusion.16
  349.1 4.2 collective-permute-start
  353.3 2.1 collective-permute-start.1
  356.3 2.4 collective-permute-start.2
  358.7 1.9 collective-permute-start.3
  366.7 3.0 copy.17
  369.7 3.7 multiply_reduce_fusion
  374.5 1.6 fusion.13
  376.1 67.2 %all-gather.11.cloned.1.call-done = bf16[256,5376]{0,1:T(8,128)(2,1)} async-done(((bf16[256,168]{0,1:T(8,128)(2,1)}), bf16[256,5376]{0,1:T(8,128)(2,1)}) %all-gather.11.cloned.1.call-update) | async-done | bytes 2752528 | tf_op jit(solution)/shard_map/all_gather | solution.py:100
  443.3 4.2 convolution_convert_fusion
  448.2 92.8 %reduce-scatter.2.cloned.1.call-done = bf16[256,336]{0,1:T(8,128)(2,1)} async-done(((bf16[256,5376]{0,1:T(8,128)(2,1)}), bf16[256,336]{0,1:T(8,128)(2,1)}) %reduce-scatter.2.cloned.1.call-update) | async-done | bytes 172048 | tf_op jit(solution)/shard_map/reduce_scatter | solution.py:103
  542.0 40.5 %psum.7 = f32[256]{0:T(256)S(1)} all-reduce(f32[256]{0:T(256)S(1)} %fusion.17), channel_id=1, replica_groups=mesh['seq'=32,'tensor'=16] {'tensor'}, use_global_device_ids=true, to_apply=%region_7.8 | all-reduce | flops 256 | bytes 2048 | tf_op jit(solution)/shard_map/psum | solution.py:106
  582.6 1.7 fusion.20
  (72 shorter events, 14.2 us)
Async XLA Ops:
  6.5 160.8 %all-gather.5.cloned.1.call-start = ((), (), s32[]{:S(2)}) async-start(), calls=%async_computation.2 | async-start | bytes 2924544 | tf_op jit(solution)/shard_map/all_gather | solution.py:61
  7.3 248.5 %all-gather.9.cloned.1.call-start = ((), (), s32[]{:S(2)}) async-start(), calls=%async_computation.4 | async-start | bytes 1419264 | tf_op jit(solution)/shard_map/all_gather | solution.py:68
  8.0 337.2 %all-gather.7.cloned.1.call-start = ((), (), s32[]{:S(2)}) async-start(), calls=%async_computation.3 | async-start | bytes 1419264 | tf_op jit(solution)/shard_map/all_gather | solution.py:69
  11.4 16.6 %copy-start.6 = (s32[256]{0:T(256)S(1)}, s32[256]{0:T(256)}, u32[]{:S(2)}) copy-start(s32[256]{0:T(256)} %param.11) | copy-start | bytes 3076
  11.4 16.7 %copy-start.8 = (f32[128]{0:T(128)S(1)}, f32[128]{0:T(128)}, u32[]{:S(2)}) copy-start(f32[128]{0:T(128)} %param.17) | copy-start | bytes 1540
  11.4 16.7 %copy-start.9 = (f32[128]{0:T(128)S(1)}, f32[128]{0:T(128)}, u32[]{:S(2)}) copy-start(f32[128]{0:T(128)} %param.16) | copy-start | bytes 1540
  11.4 16.7 %copy-start.1 = (f32[5376]{0:T(1024)S(1)}, f32[5376]{0:T(1024)}, u32[]{:S(2)}) copy-start(f32[5376]{0:T(1024)} %param.12) | copy-start | bytes 64516
  11.4 355.4 %all-to-all-start = ((bf16[32,168,256]{2,1,0:T(8,128)(2,1)}), bf16[32,168,256]{2,1,0:T(8,128)(2,1)S(1)}, u32[]{:S(2)}, u32[]{:S(2)}) async-start(bf16[32,168,256]{2,1,0:T(8,128)(2,1)} %stack.2), calls=%async_computation | async-start | bytes 5505024 | tf_op jit(solution)/shard_map/all_to_all | solution.py:16
  27.3 416.0 %all-gather.11.cloned.1.call-start = ((), (), s32[]{:S(2)}) async-start(), calls=%async_computation.5 | async-start | bytes 2838528 | tf_op jit(solution)/shard_map/all_gather | solution.py:100
  27.9 513.2 %reduce-scatter.2.cloned.1.call-start = ((), (), s32[]{:S(2)}) async-start(), calls=%async_computation.6 | async-start | bytes 2924544 | tf_op jit(solution)/shard_map/reduce_scatter | solution.py:103
  28.1 231.2 %copy-start.2 = (f32[5376]{0:T(1024)}, f32[5376]{0:T(1024)S(1)}, u32[]{:S(2)}) copy-start(f32[5376]{0:T(1024)S(1)} %broadcast_add_fusion) | copy-start | bytes 64516
  259.7 93.6 %collective-permute-start.4 = (bf16[256,1,128]{0,2,1:T(8,128)(2,1)S(1)}, bf16[256,1,128]{0,2,1:T(8,128)(2,1)}, u32[]{:S(2)}, u32[]{:S(2)}) collective-permute-start(bf16[256,1,128]{0,2,1:T(8,128)(2,1)S(1)} %pad_maximum_fusion), channel_id=1, source_target_pairs={{0,64},{16,80},{32,96},{48,112},{64,128},{80,144},{96,160},{112,17... | collective-permute-start | bytes 196616 | tf_op jit(solution)/shard_map/ppermute | solution.py:23
  264.0 92.3 %collective-permute-start.5 = (bf16[256,1,128]{0,2,1:T(8,128)(2,1)S(1)}, bf16[256,1,128]{0,2,1:T(8,128)(2,1)S(1)}, u32[]{:S(2)}, u32[]{:S(2)}) collective-permute-start(bf16[256,1,128]{0,2,1:T(8,128)(2,1)S(1)} %pad_maximum_fusion), channel_id=1, source_target_pairs={{0,48},{16,64},{32,80},{48,96},{64,112},{80,128},{96,144},{112,160... | collective-permute-start | bytes 196616 | tf_op jit(solution)/shard_map/ppermute | solution.py:23
  266.1 92.6 %collective-permute-start.6 = (bf16[256,1,128]{0,2,1:T(8,128)(2,1)S(1)}, bf16[256,1,128]{0,2,1:T(8,128)(2,1)S(1)}, u32[]{:S(2)}, u32[]{:S(2)}) collective-permute-start(bf16[256,1,128]{0,2,1:T(8,128)(2,1)S(1)} %pad_maximum_fusion), channel_id=1, source_target_pairs={{0,32},{16,48},{32,64},{48,80},{64,96},{80,112},{96,128},{112,144}... | collective-permute-start | bytes 196616 | tf_op jit(solution)/shard_map/ppermute | solution.py:23
  268.4 92.2 %collective-permute-start.7 = (bf16[256,1,128]{0,2,1:T(8,128)(2,1)S(1)}, bf16[256,1,128]{0,2,1:T(8,128)(2,1)S(1)}, u32[]{:S(2)}, u32[]{:S(2)}) collective-permute-start(bf16[256,1,128]{0,2,1:T(8,128)(2,1)S(1)} %pad_maximum_fusion), channel_id=1, source_target_pairs={{0,16},{16,32},{32,48},{48,64},{64,80},{80,96},{96,112},{112,128},... | collective-permute-start | bytes 196616 | tf_op jit(solution)/shard_map/ppermute | solution.py:23
  349.1 11.6 %collective-permute-start = (bf16[256,1,128]{2,0,1:T(8,128)(2,1)S(1)}, bf16[256,1,128]{2,0,1:T(8,128)(2,1)S(1)}, u32[]{:S(2)}, u32[]{:S(2)}) collective-permute-start(bf16[256,1,128]{2,0,1:T(8,128)(2,1)S(1)} %fusion.16), channel_id=1, source_target_pairs={{0,64},{16,80},{32,96},{48,112},{64,128},{80,144},{96,160},{112,17... | collective-permute-start | bytes 196616 | tf_op jit(solution)/shard_map/ppermute | solution.py:23
  353.3 8.3 %collective-permute-start.1 = (bf16[256,1,128]{2,0,1:T(8,128)(2,1)S(1)}, bf16[256,1,128]{2,0,1:T(8,128)(2,1)S(1)}, u32[]{:S(2)}, u32[]{:S(2)}) collective-permute-start(bf16[256,1,128]{2,0,1:T(8,128)(2,1)S(1)} %fusion.16), channel_id=1, source_target_pairs={{0,48},{16,64},{32,80},{48,96},{64,112},{80,128},{96,144},{112,160... | collective-permute-start | bytes 196616 | tf_op jit(solution)/shard_map/ppermute | solution.py:23
  356.3 7.6 %collective-permute-start.2 = (bf16[256,1,128]{2,0,1:T(8,128)(2,1)S(1)}, bf16[256,1,128]{2,0,1:T(8,128)(2,1)S(1)}, u32[]{:S(2)}, u32[]{:S(2)}) collective-permute-start(bf16[256,1,128]{2,0,1:T(8,128)(2,1)S(1)} %fusion.16), channel_id=1, source_target_pairs={{0,32},{16,48},{32,64},{48,80},{64,96},{80,112},{96,128},{112,144}... | collective-permute-start | bytes 196616 | tf_op jit(solution)/shard_map/ppermute | solution.py:23
  358.7 6.8 %collective-permute-start.3 = (bf16[256,1,128]{2,0,1:T(8,128)(2,1)S(1)}, bf16[256,1,128]{2,0,1:T(8,128)(2,1)S(1)}, u32[]{:S(2)}, u32[]{:S(2)}) collective-permute-start(bf16[256,1,128]{2,0,1:T(8,128)(2,1)S(1)} %fusion.16), channel_id=1, source_target_pairs={{0,16},{16,32},{32,48},{48,64},{64,80},{80,96},{96,112},{112,128},... | collective-permute-start | bytes 196616 | tf_op jit(solution)/shard_map/ppermute | solution.py:23
  360.6 5.4 copy-start.4
  366.7 3.0 copy-start.3
  369.7 3.9 copy-start.5
  447.6 0.7 copy-start.7
  447.6 135.0 %copy-start = (bf16[256,336]{0,1:T(8,128)(2,1)S(1)}, bf16[256,336]{0,1:T(8,128)(2,1)}, u32[]{:S(2)}) copy-start(bf16[256,336]{0,1:T(8,128)(2,1)} %param.10) | copy-start | bytes 516100
Sparse Core Ops, SparseCore 0:
  9.4 157.8 all-gather.4
  170.5 85.1 all-gather.8
  259.0 86.1 all-gather.6
  348.3 95.0 all-gather.10
  447.7 93.3 reduce-scatter.1
